TPU v7x, 32 devices: a whole 2x2x4 slice. The times are simulated.
32 devices in a mesh: particle: 8 (over z, x), band: 4 (over y, core).
Axes of the slice: x: 2, y: 2, z: 4, core: 2. Of those that a mesh axis runs over, the one named last changes fastest.
Arguments:
- states: float32 [32, 2, 64, 1024], P('particle', None, 'band'), may hold values from -4 to 4
- counts: int32 [32], replicated, may hold values from 0 to 2, as said below
Outputs:
- forecast: float32 [32, 2, 64, 1024], P('particle', None, 'band')
Inputs may be any that keep to these rules, and one draw needn't show every extreme that they name: Counts sum to 32; particle 0 and particle 32 - 1 have count 1, and for every m the particles 2m + 1 and 2m + 2 have counts summing to 2, so each slot's ancestor is the slot itself or a particle next to it; where 2m + 2 is a multiple of 4, the pair's counts are (2, 0).
All inputs are finite; a program needn't handle non-finite values.
Results may differ from a plain program's by a relative error of at most 0.00002.
Values sent between devices are 32-bit elements; how exact they have to be, the bound alone decides.
A program may use at most 64 MiB of HBM per device.

v0:
```python
import jax
import jax.numpy as jnp
from jax import lax
from jax.sharding import PartitionSpec as P

GRID_HIERARCHY = 3
COARSE_SWEEPS = 6


smoothing_weight = 0.8
deform_term = 0.1
beta_slope = 0.5
bottom_friction_coefficient = 0.2
time_step = 0.5
meridional_weight = 1.8
zonal_weight = 0.2


def padded(cells, sides, width):
    for axis, dim in sides:
        count = lax.axis_size(axis)
        ends = count - 1
        head = lax.slice_in_dim(cells, 0, width, axis=dim)
        tail = lax.slice_in_dim(cells, cells.shape[dim] - width, cells.shape[dim], axis=dim)
        cells = jnp.concatenate(
            [
                lax.ppermute(tail, axis, [(i, (i + 1) % count) for i in range(ends)]),
                cells,
                lax.ppermute(head, axis, [((i + 1) % count, i) for i in range(ends)]),
            ],
            axis=dim,
        )
    return cells


def shifted(value, axis, steps):
    count = lax.axis_size(axis)
    first, last = (max(0, -steps), min(count, count - steps))
    return lax.ppermute(value, axis, [(source, source + steps) for source in range(first, last)])


def zero_rows(field):
    border = jnp.zeros_like(field[..., :1, :])
    return jnp.concatenate([border, field, border], axis=-2)


def strip_row_count(field):
    return padded(field, (("band", 2),), 1)


def neighbours(field, widened_field):
    across = widened_field[..., 2:, :] + widened_field[..., :-2, :]
    along = jnp.roll(field, -1, axis=-1) + jnp.roll(field, 1, axis=-1)
    return meridional_weight * across + zonal_weight * along


def smooth(field, forcing_term, diagonal_term, padder):
    applied = diagonal_term * field - neighbours(field, padder(field))
    return field + smoothing_weight * (forcing_term - applied) / diagonal_term


def restrict(field):
    leading = field.shape[:-2]
    height, breadth = (field.shape[-2], field.shape[-1])
    blocks = field.reshape(leading + (height // 2, 2, breadth // 2, 2))
    return jnp.sum(blocks, axis=(-3, -1))


def prolong(field):
    return jnp.repeat(jnp.repeat(field, 2, axis=-2), 2, axis=-1)


def diagonal_at(level):
    return 4.0 + jnp.array([0.0, deform_term], jnp.float32).reshape(2, 1, 1) * 4.0**level


def coarse_solve(forcing_term, diagonal_term, padder):
    field = smoothing_weight * forcing_term / diagonal_term
    for repeat in range(COARSE_SWEEPS - 1):
        field = smooth(field, forcing_term, diagonal_term, padder)
    return field


def coarse_level(forcing_term, diagonal_term):
    height = forcing_term.shape[2]
    whole_column = lax.all_gather(forcing_term, "band", axis=2, tiled=True)
    solved = coarse_solve(whole_column, diagonal_term, zero_rows)
    return lax.dynamic_slice_in_dim(solved, lax.axis_index("band") * height, height, 2)


def cycle(forcing_term, level):
    diagonal_term = diagonal_at(level)
    if level == GRID_HIERARCHY - 1:
        return coarse_level(forcing_term, diagonal_term)
    field = smoothing_weight * forcing_term / diagonal_term
    field = smooth(field, forcing_term, diagonal_term, strip_row_count)
    remainder = forcing_term - (diagonal_term * field - neighbours(field, strip_row_count(field)))
    field = field + prolong(cycle(restrict(remainder), level + 1))
    field = smooth(field, forcing_term, diagonal_term, strip_row_count)
    field = smooth(field, forcing_term, diagonal_term, strip_row_count)
    return field


def advance_step(potential_curl_grid, stream, padded_stream, padded_vorticity):
    stream_x = 0.5 * (jnp.roll(stream, -1, axis=-1) - jnp.roll(stream, 1, axis=-1))
    meridional_streamfunction_gradient = 0.5 * (
        padded_stream[..., 2:, :] - padded_stream[..., :-2, :]
    )
    vort_x = 0.5 * (
        jnp.roll(potential_curl_grid, -1, axis=-1) - jnp.roll(potential_curl_grid, 1, axis=-1)
    )
    vort_y = 0.5 * (padded_vorticity[..., 2:, :] - padded_vorticity[..., :-2, :])
    laplace = neighbours(stream, padded_stream) - 4.0 * stream
    drag = jnp.array([0.0, bottom_friction_coefficient], jnp.float32).reshape(2, 1, 1)
    jacobian = stream_x * vort_y - meridional_streamfunction_gradient * vort_x
    return potential_curl_grid - time_step * (jacobian + beta_slope * stream_x + drag * laplace)


def mode_sources(redrawn_ensemble):
    upper = redrawn_ensemble[:, 0]
    lower = redrawn_ensemble[:, 1]
    return -jnp.stack([0.5 * (upper + lower), 0.5 * (upper - lower)], axis=1)


def stream_of(modes):
    return jnp.stack([modes[:, 0] + modes[:, 1], modes[:, 0] - modes[:, 1]], axis=1)


def per_device(states, counts):
    group = lax.axis_index("particle")
    per_group = states.shape[0]
    totals = jnp.cumsum(counts, dtype=jnp.int32)
    slots = group * per_group + jnp.arange(per_group, dtype=jnp.int32)
    ancestor = jnp.sum(
        (totals[None, :] <= slots[:, None]).astype(jnp.int32), axis=1, dtype=jnp.int32
    )
    below_last = shifted(states[-1:], "particle", 1)
    extended = jnp.concatenate([below_last, states], axis=0)
    local_index = ancestor - (group * per_group - 1)
    redrawn_ensemble = jnp.take(extended, local_index, axis=0)
    modes = cycle(mode_sources(redrawn_ensemble), 0)
    stream = stream_of(modes)
    joined = jnp.concatenate([stream, redrawn_ensemble], axis=1)
    widened_field = padded(joined, (("band", 2),), 1)
    return advance_step(redrawn_ensemble, stream, widened_field[:, :2], widened_field[:, 2:])


def solution(mesh):
    in_specs = (P("particle", None, "band", None), P())
    out_specs = P("particle", None, "band", None)
    return jax.shard_map(
        per_device, mesh=mesh, in_specs=in_specs, out_specs=out_specs, check_vma=False
    )
```

profile of v0, /device:TPU:20, one launch (start us, length us, event | category | flops | bytes accessed | tf_op | source)
XLA Modules:
  0.0 145.6 jit_solution(16377569053915027382)
XLA Ops:
  0.0 0.9 slice.395
  0.9 3.4 %collective-permute-start = (f32[1,2,16,1024]{3,2,1,0:T(8,128)S(1)}, f32[1,2,16,1024]{3,2,1,0:T(8,128)S(1)}, u32[]{:S(2)}, u32[]{:S(2)}) collective-permute-start(f32[1,2,16,1024]{3,2,1,0:T(8,128)S(1)} %slice.395), channel_id=1, source_target_pairs={{0,4},{4,8},{8,12},{12,16},{16,20},{20,24},{24,28},{1,5},{5,9},{9,... | collective-permute-start | bytes 393224 | tf_op jit(solution)/shard_map/ppermute | solution.py:39
  4.4 0.7 copy.319
  5.3 0.2 convert_reduce_fusion
  5.5 3.5 %collective-permute-done = f32[1,2,16,1024]{3,2,1,0:T(8,128)S(1)} collective-permute-done((f32[1,2,16,1024]{3,2,1,0:T(8,128)S(1)}, f32[1,2,16,1024]{3,2,1,0:T(8,128)S(1)}, u32[]{:S(2)}, u32[]{:S(2)}) %collective-permute-start) | collective-permute-done | bytes 131104 | tf_op jit(solution)/shard_map/ppermute | solution.py:39
  9.0 1.1 pad_maximum_fusion.1
  10.1 0.6 gather_fusion
  11.0 0.2 fusion.138
  11.3 1.0 fusion.127
  12.3 1.9 %collective-permute-start.1 = (f32[4,2,1,1024]{3,2,1,0:T(1,128)S(1)}, f32[4,2,1,1024]{3,2,1,0:T(1,128)S(1)}, u32[]{:S(2)}, u32[]{:S(2)}) collective-permute-start(f32[4,2,1,1024]{3,2,1,0:T(1,128)S(1)} %get-tuple-element.39), channel_id=1, source_target_pairs={{1,0},{2,1},{3,2},{5,4},{6,5},{7,6},{9,8},{10,9},{11,10},{13,12},{... | collective-permute-start | bytes 98312 | tf_op jit(solution)/shard_map/ppermute | solution.py:29
  14.2 2.4 %collective-permute-start.2 = (f32[4,2,1,1024]{3,2,1,0:T(1,128)S(1)}, f32[4,2,1,1024]{3,2,1,0:T(1,128)S(1)}, u32[]{:S(2)}, u32[]{:S(2)}) collective-permute-start(f32[4,2,1,1024]{3,2,1,0:T(1,128)S(1)} %get-tuple-element.40), channel_id=1, source_target_pairs={{0,1},{1,2},{2,3},{4,5},{5,6},{6,7},{8,9},{9,10},{10,11},{12,13},{... | collective-permute-start | bytes 98312 | tf_op jit(solution)/shard_map/ppermute | solution.py:27
  16.7 2.7 %collective-permute-done.2 = f32[4,2,1,1024]{3,2,1,0:T(1,128)S(1)} collective-permute-done((f32[4,2,1,1024]{3,2,1,0:T(1,128)S(1)}, f32[4,2,1,1024]{3,2,1,0:T(1,128)S(1)}, u32[]{:S(2)}, u32[]{:S(2)}) %collective-permute-start.2) | collective-permute-done | bytes 32800 | tf_op jit(solution)/shard_map/ppermute | solution.py:27
  19.5 0.4 fusion.40
  19.9 0.2 fusion.135
  20.1 1.9 %collective-permute-start.3 = (f32[4,2,1,1024]{3,2,1,0:T(1,128)S(1)}, f32[4,2,1,1024]{3,2,1,0:T(1,128)S(1)}, u32[]{:S(2)}, u32[]{:S(2)}) collective-permute-start(f32[4,2,1,1024]{3,2,1,0:T(1,128)S(1)} %get-tuple-element.33), channel_id=1, source_target_pairs={{1,0},{2,1},{3,2},{5,4},{6,5},{7,6},{9,8},{10,9},{11,10},{13,12},{... | collective-permute-start | bytes 98312 | tf_op jit(solution)/shard_map/ppermute | solution.py:29
  22.1 2.4 %collective-permute-start.4 = (f32[4,2,1,1024]{3,2,1,0:T(1,128)S(1)}, f32[4,2,1,1024]{3,2,1,0:T(1,128)S(1)}, u32[]{:S(2)}, u32[]{:S(2)}) collective-permute-start(f32[4,2,1,1024]{3,2,1,0:T(1,128)S(1)} %get-tuple-element.34), channel_id=1, source_target_pairs={{0,1},{1,2},{2,3},{4,5},{5,6},{6,7},{8,9},{9,10},{10,11},{12,13},{... | collective-permute-start | bytes 98312 | tf_op jit(solution)/shard_map/ppermute | solution.py:27
  24.6 2.7 %collective-permute-done.4 = f32[4,2,1,1024]{3,2,1,0:T(1,128)S(1)} collective-permute-done((f32[4,2,1,1024]{3,2,1,0:T(1,128)S(1)}, f32[4,2,1,1024]{3,2,1,0:T(1,128)S(1)}, u32[]{:S(2)}, u32[]{:S(2)}) %collective-permute-start.4) | collective-permute-done | bytes 32800 | tf_op jit(solution)/shard_map/ppermute | solution.py:27
  27.3 0.4 fusion.32
  27.7 8.6 %copy.320 = f32[4,2,16,1024]{0,3,2,1:T(8,128)} copy(f32[4,2,16,1024]{3,2,1,0:T(8,128)S(1)} %fusion.32) | data formatting | bytes 1048576 | tf_op jit(solution)/shard_map/sub | solution.py:97
  36.3 17.7 %reduce_sum.28 = f32[4,2,8,512]{0,3,2,1:T(8,128)} reduce(f32[4,2,8,2,512,2]{0,5,4,3,2,1:T(2,128)} %bitcast.11, f32[]{:T(128)} %constant.31.clone.1), dimensions={3,5}, to_apply=%region_2.3 | reduce | flops 98304 | bytes 655364 | tf_op jit(solution)/shard_map/reduce_sum | solution.py:66
  54.0 2.9 %copy.321 = f32[4,2,8,512]{3,2,1,0:T(8,128)S(1)} copy(f32[4,2,8,512]{0,3,2,1:T(8,128)} %reduce_sum.28) | data formatting | bytes 262144 | tf_op jit(solution)/shard_map/reduce_sum | solution.py:66
  57.1 1.9 %collective-permute-start.5 = (f32[4,2,1,512]{3,0,2,1:T(4,128)S(1)}, f32[4,2,1,512]{3,0,2,1:T(4,128)S(1)}, u32[]{:S(2)}, u32[]{:S(2)}) collective-permute-start(f32[4,2,1,512]{3,0,2,1:T(4,128)S(1)} %copy.322), channel_id=1, source_target_pairs={{1,0},{2,1},{3,2},{5,4},{6,5},{7,6},{9,8},{10,9},{11,10},{13,12},{... | collective-permute-start | bytes 49160 | tf_op jit(solution)/shard_map/ppermute | solution.py:29
  59.0 2.4 %collective-permute-start.6 = (f32[4,2,1,512]{3,0,2,1:T(4,128)S(1)}, f32[4,2,1,512]{3,0,2,1:T(4,128)S(1)}, u32[]{:S(2)}, u32[]{:S(2)}) collective-permute-start(f32[4,2,1,512]{3,0,2,1:T(4,128)S(1)} %copy.324), channel_id=1, source_target_pairs={{0,1},{1,2},{2,3},{4,5},{5,6},{6,7},{8,9},{9,10},{10,11},{12,13},{... | collective-permute-start | bytes 49160 | tf_op jit(solution)/shard_map/ppermute | solution.py:27
  61.6 2.5 %collective-permute-done.6 = f32[4,2,1,512]{3,0,2,1:T(4,128)S(1)} collective-permute-done((f32[4,2,1,512]{3,0,2,1:T(4,128)S(1)}, f32[4,2,1,512]{3,0,2,1:T(4,128)S(1)}, u32[]{:S(2)}, u32[]{:S(2)}) %collective-permute-start.6) | collective-permute-done | bytes 16416 | tf_op jit(solution)/shard_map/ppermute | solution.py:27
  64.4 1.9 %collective-permute-start.7 = (f32[4,2,1,512]{3,0,2,1:T(4,128)S(1)}, f32[4,2,1,512]{3,0,2,1:T(4,128)S(1)}, u32[]{:S(2)}, u32[]{:S(2)}) collective-permute-start(f32[4,2,1,512]{3,0,2,1:T(4,128)S(1)} %copy.327), channel_id=1, source_target_pairs={{1,0},{2,1},{3,2},{5,4},{6,5},{7,6},{9,8},{10,9},{11,10},{13,12},{... | collective-permute-start | bytes 49160 | tf_op jit(solution)/shard_map/ppermute | solution.py:29
  66.4 2.4 %collective-permute-start.8 = (f32[4,2,1,512]{3,0,2,1:T(4,128)S(1)}, f32[4,2,1,512]{3,0,2,1:T(4,128)S(1)}, u32[]{:S(2)}, u32[]{:S(2)}) collective-permute-start(f32[4,2,1,512]{3,0,2,1:T(4,128)S(1)} %copy.329), channel_id=1, source_target_pairs={{0,1},{1,2},{2,3},{4,5},{5,6},{6,7},{8,9},{9,10},{10,11},{12,13},{... | collective-permute-start | bytes 49160 | tf_op jit(solution)/shard_map/ppermute | solution.py:27
  68.9 2.5 %collective-permute-done.8 = f32[4,2,1,512]{3,0,2,1:T(4,128)S(1)} collective-permute-done((f32[4,2,1,512]{3,0,2,1:T(4,128)S(1)}, f32[4,2,1,512]{3,0,2,1:T(4,128)S(1)}, u32[]{:S(2)}, u32[]{:S(2)}) %collective-permute-start.8) | collective-permute-done | bytes 16416 | tf_op jit(solution)/shard_map/ppermute | solution.py:27
  71.6 2.7 %copy.332 = f32[4,2,8,512]{0,3,2,1:T(8,128)} copy(f32[4,2,8,512]{3,2,1,0:T(8,128)S(1)} %fusion.101) | data formatting | bytes 262144 | tf_op jit(solution)/shard_map/sub | solution.py:97
  74.3 5.8 %reduce_sum.29 = f32[4,2,4,256]{0,3,2,1:T(8,128)S(1)} reduce(f32[4,2,4,2,256,2]{0,5,4,3,2,1:T(2,128)} %bitcast.13, f32[]{:T(128)} %constant.31.clone.1), dimensions={3,5}, to_apply=%region_3.4 | reduce | flops 24576 | bytes 163844 | tf_op jit(solution)/shard_map/reduce_sum | solution.py:66
  80.0 0.9 copy.333
  81.0 5.8 %all_gather.3 = f32[4,2,16,256]{3,0,1,2:T(4,128)S(1)} all-gather(f32[4,2,4,256]{3,0,1,2:T(4,128)} %copy.333), channel_id=1, replica_groups=mesh['particle'=8,'band'=4] {'band'}, dimensions={2}, use_global_device_ids=true | all-gather | bytes 163840 | tf_op jit(solution)/shard_map/all_gather | solution.py:86
  87.1 0.2 fusion.54
  87.4 0.2 fusion.62
  87.8 0.2 fusion.70
  88.1 0.2 fusion.78
  88.7 0.7 broadcast_in_dim.20
  89.4 1.2 copy.341
  90.6 2.1 %broadcast_in_dim.21 = f32[4,2,8,256,2]{2,4,3,1,0:T(2,128)} broadcast(f32[4,2,8,256]{2,3,1,0:T(8,128)S(1)} %copy.341), dimensions={0,1,2,3} | broadcast | bytes 196608 | tf_op jit(solution)/shard_map/broadcast_in_dim | solution.py:70
  92.7 2.2 %copy.342 = f32[4,2,8,512]{3,2,1,0:T(8,128)S(1)} copy(f32[4,2,8,512]{2,3,1,0:T(8,128)} %bitcast.14) | data formatting | bytes 262144 | tf_op jit(solution)/shard_map/reshape | solution.py:70
  95.0 2.0 %collective-permute-start.9 = (f32[4,2,1,512]{3,0,2,1:T(4,128)S(1)}, f32[4,2,1,512]{3,0,2,1:T(4,128)S(1)}, u32[]{:S(2)}, u32[]{:S(2)}) collective-permute-start(f32[4,2,1,512]{3,0,2,1:T(4,128)S(1)} %copy.343), channel_id=1, source_target_pairs={{1,0},{2,1},{3,2},{5,4},{6,5},{7,6},{9,8},{10,9},{11,10},{13,12},{... | collective-permute-start | bytes 49160 | tf_op jit(solution)/shard_map/ppermute | solution.py:29
  97.0 2.3 %collective-permute-start.10 = (f32[4,2,1,512]{3,0,2,1:T(4,128)S(1)}, f32[4,2,1,512]{3,0,2,1:T(4,128)S(1)}, u32[]{:S(2)}, u32[]{:S(2)}) collective-permute-start(f32[4,2,1,512]{3,0,2,1:T(4,128)S(1)} %copy.345), channel_id=1, source_target_pairs={{0,1},{1,2},{2,3},{4,5},{5,6},{6,7},{8,9},{9,10},{10,11},{12,13},{... | collective-permute-start | bytes 49160 | tf_op jit(solution)/shard_map/ppermute | solution.py:27
  99.5 2.6 %collective-permute-done.10 = f32[4,2,1,512]{3,0,2,1:T(4,128)S(1)} collective-permute-done((f32[4,2,1,512]{3,0,2,1:T(4,128)S(1)}, f32[4,2,1,512]{3,0,2,1:T(4,128)S(1)}, u32[]{:S(2)}, u32[]{:S(2)}) %collective-permute-start.10) | collective-permute-done | bytes 16416 | tf_op jit(solution)/shard_map/ppermute | solution.py:27
  102.1 0.8 fusion.96
  103.1 1.9 %collective-permute-start.11 = (f32[4,2,1,512]{3,0,2,1:T(4,128)S(1)}, f32[4,2,1,512]{3,0,2,1:T(4,128)S(1)}, u32[]{:S(2)}, u32[]{:S(2)}) collective-permute-start(f32[4,2,1,512]{3,0,2,1:T(4,128)S(1)} %copy.348), channel_id=1, source_target_pairs={{1,0},{2,1},{3,2},{5,4},{6,5},{7,6},{9,8},{10,9},{11,10},{13,12},{... | collective-permute-start | bytes 49160 | tf_op jit(solution)/shard_map/ppermute | solution.py:29
  105.0 2.4 %collective-permute-start.12 = (f32[4,2,1,512]{3,0,2,1:T(4,128)S(1)}, f32[4,2,1,512]{3,0,2,1:T(4,128)S(1)}, u32[]{:S(2)}, u32[]{:S(2)}) collective-permute-start(f32[4,2,1,512]{3,0,2,1:T(4,128)S(1)} %copy.350), channel_id=1, source_target_pairs={{0,1},{1,2},{2,3},{4,5},{5,6},{6,7},{8,9},{9,10},{10,11},{12,13},{... | collective-permute-start | bytes 49160 | tf_op jit(solution)/shard_map/ppermute | solution.py:27
  107.5 2.5 %collective-permute-done.12 = f32[4,2,1,512]{3,0,2,1:T(4,128)S(1)} collective-permute-done((f32[4,2,1,512]{3,0,2,1:T(4,128)S(1)}, f32[4,2,1,512]{3,0,2,1:T(4,128)S(1)}, u32[]{:S(2)}, u32[]{:S(2)}) %collective-permute-start.12) | collective-permute-done | bytes 16416 | tf_op jit(solution)/shard_map/ppermute | solution.py:27
  110.4 2.0 %copy.354 = f32[4,2,16,512]{2,3,1,0:T(8,128)} copy(f32[4,2,16,512]{3,1,2,0:T(2,128)S(1)} %bitcast.15) | data formatting | bytes 524288 | tf_op jit(solution)/shard_map/reshape | solution.py:70
  112.4 5.0 %broadcast_in_dim.23 = f32[4,2,16,512,2]{2,4,3,1,0:T(2,128)} broadcast(f32[4,2,16,512]{2,3,1,0:T(8,128)} %copy.354), dimensions={0,1,2,3} | broadcast | bytes 786432 | tf_op jit(solution)/shard_map/broadcast_in_dim | solution.py:70
  117.4 2.8 %copy.355 = f32[4,2,16,1024]{3,2,1,0:T(8,128)S(1)} copy(f32[4,2,16,1024]{2,3,1,0:T(8,128)} %bitcast.12) | data formatting | bytes 1048576 | tf_op jit(solution)/shard_map/reshape | solution.py:70
  120.3 0.2 fusion.132
  120.5 1.9 %collective-permute-start.13 = (f32[4,2,1,1024]{3,2,1,0:T(1,128)S(1)}, f32[4,2,1,1024]{3,2,1,0:T(1,128)S(1)}, u32[]{:S(2)}, u32[]{:S(2)}) collective-permute-start(f32[4,2,1,1024]{3,2,1,0:T(1,128)S(1)} %get-tuple-element.27), channel_id=1, source_target_pairs={{1,0},{2,1},{3,2},{5,4},{6,5},{7,6},{9,8},{10,9},{11,10},{13,12},{... | collective-permute-start | bytes 98312 | tf_op jit(solution)/shard_map/ppermute | solution.py:29
  122.5 2.4 %collective-permute-start.14 = (f32[4,2,1,1024]{3,2,1,0:T(1,128)S(1)}, f32[4,2,1,1024]{3,2,1,0:T(1,128)S(1)}, u32[]{:S(2)}, u32[]{:S(2)}) collective-permute-start(f32[4,2,1,1024]{3,2,1,0:T(1,128)S(1)} %get-tuple-element.28), channel_id=1, source_target_pairs={{0,1},{1,2},{2,3},{4,5},{5,6},{6,7},{8,9},{9,10},{10,11},{12,13},{... | collective-permute-start | bytes 98312 | tf_op jit(solution)/shard_map/ppermute | solution.py:27
  125.0 2.7 %collective-permute-done.14 = f32[4,2,1,1024]{3,2,1,0:T(1,128)S(1)} collective-permute-done((f32[4,2,1,1024]{3,2,1,0:T(1,128)S(1)}, f32[4,2,1,1024]{3,2,1,0:T(1,128)S(1)}, u32[]{:S(2)}, u32[]{:S(2)}) %collective-permute-start.14) | collective-permute-done | bytes 32800 | tf_op jit(solution)/shard_map/ppermute | solution.py:27
  127.7 0.4 fusion.27
  128.1 0.2 fusion.129
  128.4 2.1 %collective-permute-start.15 = (f32[4,2,1,1024]{3,2,1,0:T(1,128)S(1)}, f32[4,2,1,1024]{3,2,1,0:T(1,128)S(1)}, u32[]{:S(2)}, u32[]{:S(2)}) collective-permute-start(f32[4,2,1,1024]{3,2,1,0:T(1,128)S(1)} %get-tuple-element.21), channel_id=1, source_target_pairs={{1,0},{2,1},{3,2},{5,4},{6,5},{7,6},{9,8},{10,9},{11,10},{13,12},{... | collective-permute-start | bytes 98312 | tf_op jit(solution)/shard_map/ppermute | solution.py:29
  130.5 2.4 %collective-permute-start.16 = (f32[4,2,1,1024]{3,2,1,0:T(1,128)S(1)}, f32[4,2,1,1024]{3,2,1,0:T(1,128)S(1)}, u32[]{:S(2)}, u32[]{:S(2)}) collective-permute-start(f32[4,2,1,1024]{3,2,1,0:T(1,128)S(1)} %get-tuple-element.22), channel_id=1, source_target_pairs={{0,1},{1,2},{2,3},{4,5},{5,6},{6,7},{8,9},{9,10},{10,11},{12,13},{... | collective-permute-start | bytes 98312 | tf_op jit(solution)/shard_map/ppermute | solution.py:27
  133.0 2.7 %collective-permute-done.16 = f32[4,2,1,1024]{3,2,1,0:T(1,128)S(1)} collective-permute-done((f32[4,2,1,1024]{3,2,1,0:T(1,128)S(1)}, f32[4,2,1,1024]{3,2,1,0:T(1,128)S(1)}, u32[]{:S(2)}, u32[]{:S(2)}) %collective-permute-start.16) | collective-permute-done | bytes 32800 | tf_op jit(solution)/shard_map/ppermute | solution.py:27
  135.7 0.4 fusion.19
  136.2 0.2 fusion
  136.5 1.9 %collective-permute-start.17 = (f32[4,4,1,1024]{3,2,1,0:T(1,128)S(1)}, f32[4,4,1,1024]{3,2,1,0:T(1,128)S(1)}, u32[]{:S(2)}, u32[]{:S(2)}) collective-permute-start(f32[4,4,1,1024]{3,2,1,0:T(1,128)S(1)} %get-tuple-element.5), channel_id=1, source_target_pairs={{1,0},{2,1},{3,2},{5,4},{6,5},{7,6},{9,8},{10,9},{11,10},{13,12},{... | collective-permute-start | bytes 196616 | tf_op jit(solution)/shard_map/ppermute | solution.py:29
  138.4 2.4 %collective-permute-start.18 = (f32[4,4,1,1024]{3,2,1,0:T(1,128)S(1)}, f32[4,4,1,1024]{3,2,1,0:T(1,128)S(1)}, u32[]{:S(2)}, u32[]{:S(2)}) collective-permute-start(f32[4,4,1,1024]{3,2,1,0:T(1,128)S(1)} %get-tuple-element.6), channel_id=1, source_target_pairs={{0,1},{1,2},{2,3},{4,5},{5,6},{6,7},{8,9},{9,10},{10,11},{12,13},{... | collective-permute-start | bytes 196616 | tf_op jit(solution)/shard_map/ppermute | solution.py:27
  140.9 3.1 %collective-permute-done.18 = f32[4,4,1,1024]{3,2,1,0:T(1,128)S(1)} collective-permute-done((f32[4,4,1,1024]{3,2,1,0:T(1,128)S(1)}, f32[4,4,1,1024]{3,2,1,0:T(1,128)S(1)}, u32[]{:S(2)}, u32[]{:S(2)}) %collective-permute-start.18) | collective-permute-done | bytes 65568 | tf_op jit(solution)/shard_map/ppermute | solution.py:27
  144.0 1.5 %fusion.7 = f32[4,2,16,1024]{3,2,1,0:T(8,128)} fusion(f32[4,2,16,1024]{3,2,1,0:T(8,128)S(1)} %broadcast_select_fusion, f32[4,1,16,1024]{3,2,1,0:T(8,128)S(1)} %get-tuple-element.16, f32[4,1,16,1024]{3,2,1,0:T(8,128)S(1)} %get-tuple-element.15, f32[4,4,1,1024]{3,2,1,0:T(1,128)S(1)} %collective-permute-done.18, ...), kind=kLoop, calls=%fused_computation.18 | loop fusion | flops 5373952 | bytes 3801096 | tf_op jit(solution)/shard_map/sub | solution.py:116
  (100 shorter events, 4.2 us)
Async XLA Ops:
  0.0 10.8 %copy-start.3 = (f32[2]{0:T(128)S(1)}, f32[2]{0:T(128)}, u32[]{:S(2)}) copy-start(f32[2]{0:T(128)} %constant.92) | copy-start | bytes 28
  0.9 8.0 %collective-permute-start = (f32[1,2,16,1024]{3,2,1,0:T(8,128)S(1)}, f32[1,2,16,1024]{3,2,1,0:T(8,128)S(1)}, u32[]{:S(2)}, u32[]{:S(2)}) collective-permute-start(f32[1,2,16,1024]{3,2,1,0:T(8,128)S(1)} %slice.395), channel_id=1, source_target_pairs={{0,4},{4,8},{8,12},{12,16},{16,20},{20,24},{24,28},{1,5},{5,9},{9,... | collective-permute-start | bytes 393224 | tf_op jit(solution)/shard_map/ppermute | solution.py:39
  10.6 8.8 %copy-start.4 = (f32[2]{0:T(128)S(1)}, f32[2]{0:T(128)}, u32[]{:S(2)}) copy-start(f32[2]{0:T(128)} %constant.87) | copy-start | bytes 28
  12.3 4.4 %collective-permute-start.1 = (f32[4,2,1,1024]{3,2,1,0:T(1,128)S(1)}, f32[4,2,1,1024]{3,2,1,0:T(1,128)S(1)}, u32[]{:S(2)}, u32[]{:S(2)}) collective-permute-start(f32[4,2,1,1024]{3,2,1,0:T(1,128)S(1)} %get-tuple-element.39), channel_id=1, source_target_pairs={{1,0},{2,1},{3,2},{5,4},{6,5},{7,6},{9,8},{10,9},{11,10},{13,12},{... | collective-permute-start | bytes 98312 | tf_op jit(solution)/shard_map/ppermute | solution.py:29
  14.2 5.2 %collective-permute-start.2 = (f32[4,2,1,1024]{3,2,1,0:T(1,128)S(1)}, f32[4,2,1,1024]{3,2,1,0:T(1,128)S(1)}, u32[]{:S(2)}, u32[]{:S(2)}) collective-permute-start(f32[4,2,1,1024]{3,2,1,0:T(1,128)S(1)} %get-tuple-element.40), channel_id=1, source_target_pairs={{0,1},{1,2},{2,3},{4,5},{5,6},{6,7},{8,9},{9,10},{10,11},{12,13},{... | collective-permute-start | bytes 98312 | tf_op jit(solution)/shard_map/ppermute | solution.py:27
  20.1 4.4 %collective-permute-start.3 = (f32[4,2,1,1024]{3,2,1,0:T(1,128)S(1)}, f32[4,2,1,1024]{3,2,1,0:T(1,128)S(1)}, u32[]{:S(2)}, u32[]{:S(2)}) collective-permute-start(f32[4,2,1,1024]{3,2,1,0:T(1,128)S(1)} %get-tuple-element.33), channel_id=1, source_target_pairs={{1,0},{2,1},{3,2},{5,4},{6,5},{7,6},{9,8},{10,9},{11,10},{13,12},{... | collective-permute-start | bytes 98312 | tf_op jit(solution)/shard_map/ppermute | solution.py:29
  22.1 5.2 %collective-permute-start.4 = (f32[4,2,1,1024]{3,2,1,0:T(1,128)S(1)}, f32[4,2,1,1024]{3,2,1,0:T(1,128)S(1)}, u32[]{:S(2)}, u32[]{:S(2)}) collective-permute-start(f32[4,2,1,1024]{3,2,1,0:T(1,128)S(1)} %get-tuple-element.34), channel_id=1, source_target_pairs={{0,1},{1,2},{2,3},{4,5},{5,6},{6,7},{8,9},{9,10},{10,11},{12,13},{... | collective-permute-start | bytes 98312 | tf_op jit(solution)/shard_map/ppermute | solution.py:27
  54.0 2.9 %copy-start.5 = (f32[2]{0:T(128)S(1)}, f32[2]{0:T(128)}, u32[]{:S(2)}) copy-start(f32[2]{0:T(128)} %constant.94) | copy-start | bytes 28
  54.0 10.2 %copy-start.7 = (f32[2]{0:T(128)S(1)}, f32[2]{0:T(128)}, u32[]{:S(2)}) copy-start(f32[2]{0:T(128)} %constant.89) | copy-start | bytes 28
  57.1 4.4 %collective-permute-start.5 = (f32[4,2,1,512]{3,0,2,1:T(4,128)S(1)}, f32[4,2,1,512]{3,0,2,1:T(4,128)S(1)}, u32[]{:S(2)}, u32[]{:S(2)}) collective-permute-start(f32[4,2,1,512]{3,0,2,1:T(4,128)S(1)} %copy.322), channel_id=1, source_target_pairs={{1,0},{2,1},{3,2},{5,4},{6,5},{7,6},{9,8},{10,9},{11,10},{13,12},{... | collective-permute-start | bytes 49160 | tf_op jit(solution)/shard_map/ppermute | solution.py:29
  59.0 5.1 %collective-permute-start.6 = (f32[4,2,1,512]{3,0,2,1:T(4,128)S(1)}, f32[4,2,1,512]{3,0,2,1:T(4,128)S(1)}, u32[]{:S(2)}, u32[]{:S(2)}) collective-permute-start(f32[4,2,1,512]{3,0,2,1:T(4,128)S(1)} %copy.324), channel_id=1, source_target_pairs={{0,1},{1,2},{2,3},{4,5},{5,6},{6,7},{8,9},{9,10},{10,11},{12,13},{... | collective-permute-start | bytes 49160 | tf_op jit(solution)/shard_map/ppermute | solution.py:27
  64.4 4.4 %collective-permute-start.7 = (f32[4,2,1,512]{3,0,2,1:T(4,128)S(1)}, f32[4,2,1,512]{3,0,2,1:T(4,128)S(1)}, u32[]{:S(2)}, u32[]{:S(2)}) collective-permute-start(f32[4,2,1,512]{3,0,2,1:T(4,128)S(1)} %copy.327), channel_id=1, source_target_pairs={{1,0},{2,1},{3,2},{5,4},{6,5},{7,6},{9,8},{10,9},{11,10},{13,12},{... | collective-permute-start | bytes 49160 | tf_op jit(solution)/shard_map/ppermute | solution.py:29
  66.4 5.1 %collective-permute-start.8 = (f32[4,2,1,512]{3,0,2,1:T(4,128)S(1)}, f32[4,2,1,512]{3,0,2,1:T(4,128)S(1)}, u32[]{:S(2)}, u32[]{:S(2)}) collective-permute-start(f32[4,2,1,512]{3,0,2,1:T(4,128)S(1)} %copy.329), channel_id=1, source_target_pairs={{0,1},{1,2},{2,3},{4,5},{5,6},{6,7},{8,9},{9,10},{10,11},{12,13},{... | collective-permute-start | bytes 49160 | tf_op jit(solution)/shard_map/ppermute | solution.py:27
  74.3 12.5 %copy-start.1 = (f32[2]{0:T(128)S(1)}, f32[2]{0:T(128)}, u32[]{:S(2)}) copy-start(f32[2]{0:T(128)} %constant.96) | copy-start | bytes 28
  74.3 12.8 %copy-start.2 = (f32[2]{0:T(128)S(1)}, f32[2]{0:T(128)}, u32[]{:S(2)}) copy-start(f32[2]{0:T(128)} %constant.91) | copy-start | bytes 28
  90.6 19.5 %copy-start.6 = (f32[2]{0:T(128)S(1)}, f32[2]{0:T(128)}, u32[]{:S(2)}) copy-start(f32[2]{0:T(128)} %constant.94) | copy-start | bytes 28
  90.6 19.5 %copy-start.8 = (f32[2]{0:T(128)S(1)}, f32[2]{0:T(128)}, u32[]{:S(2)}) copy-start(f32[2]{0:T(128)} %constant.89) | copy-start | bytes 28
  95.0 4.4 %collective-permute-start.9 = (f32[4,2,1,512]{3,0,2,1:T(4,128)S(1)}, f32[4,2,1,512]{3,0,2,1:T(4,128)S(1)}, u32[]{:S(2)}, u32[]{:S(2)}) collective-permute-start(f32[4,2,1,512]{3,0,2,1:T(4,128)S(1)} %copy.343), channel_id=1, source_target_pairs={{1,0},{2,1},{3,2},{5,4},{6,5},{7,6},{9,8},{10,9},{11,10},{13,12},{... | collective-permute-start | bytes 49160 | tf_op jit(solution)/shard_map/ppermute | solution.py:29
  97.0 5.1 %collective-permute-start.10 = (f32[4,2,1,512]{3,0,2,1:T(4,128)S(1)}, f32[4,2,1,512]{3,0,2,1:T(4,128)S(1)}, u32[]{:S(2)}, u32[]{:S(2)}) collective-permute-start(f32[4,2,1,512]{3,0,2,1:T(4,128)S(1)} %copy.345), channel_id=1, source_target_pairs={{0,1},{1,2},{2,3},{4,5},{5,6},{6,7},{8,9},{9,10},{10,11},{12,13},{... | collective-permute-start | bytes 49160 | tf_op jit(solution)/shard_map/ppermute | solution.py:27
  103.1 4.4 %collective-permute-start.11 = (f32[4,2,1,512]{3,0,2,1:T(4,128)S(1)}, f32[4,2,1,512]{3,0,2,1:T(4,128)S(1)}, u32[]{:S(2)}, u32[]{:S(2)}) collective-permute-start(f32[4,2,1,512]{3,0,2,1:T(4,128)S(1)} %copy.348), channel_id=1, source_target_pairs={{1,0},{2,1},{3,2},{5,4},{6,5},{7,6},{9,8},{10,9},{11,10},{13,12},{... | collective-permute-start | bytes 49160 | tf_op jit(solution)/shard_map/ppermute | solution.py:29
  105.0 5.1 %collective-permute-start.12 = (f32[4,2,1,512]{3,0,2,1:T(4,128)S(1)}, f32[4,2,1,512]{3,0,2,1:T(4,128)S(1)}, u32[]{:S(2)}, u32[]{:S(2)}) collective-permute-start(f32[4,2,1,512]{3,0,2,1:T(4,128)S(1)} %copy.350), channel_id=1, source_target_pairs={{0,1},{1,2},{2,3},{4,5},{5,6},{6,7},{8,9},{9,10},{10,11},{12,13},{... | collective-permute-start | bytes 49160 | tf_op jit(solution)/shard_map/ppermute | solution.py:27
  120.5 4.4 %collective-permute-start.13 = (f32[4,2,1,1024]{3,2,1,0:T(1,128)S(1)}, f32[4,2,1,1024]{3,2,1,0:T(1,128)S(1)}, u32[]{:S(2)}, u32[]{:S(2)}) collective-permute-start(f32[4,2,1,1024]{3,2,1,0:T(1,128)S(1)} %get-tuple-element.27), channel_id=1, source_target_pairs={{1,0},{2,1},{3,2},{5,4},{6,5},{7,6},{9,8},{10,9},{11,10},{13,12},{... | collective-permute-start | bytes 98312 | tf_op jit(solution)/shard_map/ppermute | solution.py:29
  122.5 5.2 %collective-permute-start.14 = (f32[4,2,1,1024]{3,2,1,0:T(1,128)S(1)}, f32[4,2,1,1024]{3,2,1,0:T(1,128)S(1)}, u32[]{:S(2)}, u32[]{:S(2)}) collective-permute-start(f32[4,2,1,1024]{3,2,1,0:T(1,128)S(1)} %get-tuple-element.28), channel_id=1, source_target_pairs={{0,1},{1,2},{2,3},{4,5},{5,6},{6,7},{8,9},{9,10},{10,11},{12,13},{... | collective-permute-start | bytes 98312 | tf_op jit(solution)/shard_map/ppermute | solution.py:27
  128.3 15.7 %copy-start = (f32[4,2,16,1023]{3,2,1,0:T(8,128)S(1)}, f32[4,2,16,1023]{3,2,1,0:T(8,128)}, u32[]{:S(2)}) copy-start(f32[4,2,16,1023]{3,2,1,0:T(8,128)} %get-tuple-element.14) | copy-start | bytes 1571332
  128.3 15.7 %copy-start.9 = (f32[2]{0:T(128)S(1)}, f32[2]{0:T(128)}, u32[]{:S(2)}) copy-start(f32[2]{0:T(128)} %constant.65.clone) | copy-start | bytes 28
  128.4 4.6 %collective-permute-start.15 = (f32[4,2,1,1024]{3,2,1,0:T(1,128)S(1)}, f32[4,2,1,1024]{3,2,1,0:T(1,128)S(1)}, u32[]{:S(2)}, u32[]{:S(2)}) collective-permute-start(f32[4,2,1,1024]{3,2,1,0:T(1,128)S(1)} %get-tuple-element.21), channel_id=1, source_target_pairs={{1,0},{2,1},{3,2},{5,4},{6,5},{7,6},{9,8},{10,9},{11,10},{13,12},{... | collective-permute-start | bytes 98312 | tf_op jit(solution)/shard_map/ppermute | solution.py:29
  130.5 5.2 %collective-permute-start.16 = (f32[4,2,1,1024]{3,2,1,0:T(1,128)S(1)}, f32[4,2,1,1024]{3,2,1,0:T(1,128)S(1)}, u32[]{:S(2)}, u32[]{:S(2)}) collective-permute-start(f32[4,2,1,1024]{3,2,1,0:T(1,128)S(1)} %get-tuple-element.22), channel_id=1, source_target_pairs={{0,1},{1,2},{2,3},{4,5},{5,6},{6,7},{8,9},{9,10},{10,11},{12,13},{... | collective-permute-start | bytes 98312 | tf_op jit(solution)/shard_map/ppermute | solution.py:27
  136.5 4.4 %collective-permute-start.17 = (f32[4,4,1,1024]{3,2,1,0:T(1,128)S(1)}, f32[4,4,1,1024]{3,2,1,0:T(1,128)S(1)}, u32[]{:S(2)}, u32[]{:S(2)}) collective-permute-start(f32[4,4,1,1024]{3,2,1,0:T(1,128)S(1)} %get-tuple-element.5), channel_id=1, source_target_pairs={{1,0},{2,1},{3,2},{5,4},{6,5},{7,6},{9,8},{10,9},{11,10},{13,12},{... | collective-permute-start | bytes 196616 | tf_op jit(solution)/shard_map/ppermute | solution.py:29
  138.4 5.6 %collective-permute-start.18 = (f32[4,4,1,1024]{3,2,1,0:T(1,128)S(1)}, f32[4,4,1,1024]{3,2,1,0:T(1,128)S(1)}, u32[]{:S(2)}, u32[]{:S(2)}) collective-permute-start(f32[4,4,1,1024]{3,2,1,0:T(1,128)S(1)} %get-tuple-element.6), channel_id=1, source_target_pairs={{0,1},{1,2},{2,3},{4,5},{5,6},{6,7},{8,9},{9,10},{10,11},{12,13},{... | collective-permute-start | bytes 196616 | tf_op jit(solution)/shard_map/ppermute | solution.py:27
where the time goes:
time: 146 us
  starting transfers between devices  42.4 us (29%)
  local copies, waits for them, and re-layouts  37.7 us (26%)
  other arithmetic  31.1 us (21%)
  waiting for transfers between devices  27.8 us (19%)
  blocking collectives  5.8 us (4%)
    ppermute x9, waiting for transfers between devices, padded(): lax.ppermute(tail, axis, [(i, (i + 1) % count) for i in range(ends)])  24.3 us
    reduce_sum x2, other arithmetic, restrict(): return jnp.sum(blocks, axis=(-3, -1))  23.4 us
    ppermute x9, starting transfers between devices, padded(): lax.ppermute(tail, axis, [(i, (i + 1) % count) for i in range(ends)])  21.6 us
    ppermute x9, starting transfers between devices, padded(): lax.ppermute(head, axis, [((i + 1) % count, i) for i in range(ends)])  17.5 us
    sub x2, local copies, waits for them, and re-layouts, cycle(): forcing_term - (diagonal_term * field - neighbours(field, strip_row_count...  11.3 us
    reshape x4, local copies, waits for them, and re-layouts, prolong(): return jnp.repeat(jnp.repeat(field, 2, axis=-2), 2, axis=-1)  8.08 us
    broadcast_in_dim x4, local copies, waits for them, and re-layouts, prolong(): return jnp.repeat(jnp.repeat(field, 2, axis=-2), 2, axis=-1)  7.81 us
    all_gather x1, blocking collectives, coarse_level(): whole_column = lax.all_gather(forcing_term, 'band', axis=2, tiled=True)  5.8 us
  transfers between devices with their start and end apart: 19, of which 10 were waited for; matrix products, arithmetic and copies ran while one was open for 1% of the time, Pallas kernels for 0%

commit v1 on v0

v1 whole, which is shorter than its diff:
```python
import functools

import jax
import jax.numpy as jnp
from jax import lax
from jax.experimental import pallas as pl
from jax.experimental.pallas import tpu as pltpu
from jax.sharding import PartitionSpec as P

MESH = pl.DeviceIdType.MESH
DEFORM = 0.1
RELAX = 0.8
BETA = 0.5
DRAG = 0.2
STEP = 0.5
WY = 1.8
WX = 0.2
H0 = 6
H1 = 5
HC = 8


def lane_roll(a, steps):
    return pltpu.roll(a, steps % a.shape[-1], axis=a.ndim - 1)


def sides(row):
    n = len(row)
    left = [row[r - 1] if r else lane_roll(row[n - 1], 1) for r in range(n)]
    right = [row[r + 1] if r < n - 1 else lane_roll(row[0], -1) for r in range(n)]
    return left, right


def nb(above, row, below):
    left, right = sides(row)
    return [
        WY * (above[r] + below[r]) + WX * (left[r] + right[r]) for r in range(len(row))
    ]


def kernel(bands, groups, slots, rows, counts, x_hbm, out_hbm,
           xv, ov, fwd, inv, tr, q, s0, f0, g0, h0, s1, f1, g1, h1, s2, c2a, c2b,
           in_sem, out_sem, send_sem, recv_sem):
    band = lax.axis_index("band")
    group = lax.axis_index("particle")
    rows1, rows2 = rows // 2, rows // 4
    has = [band >= 1, band >= 2, band < bands - 1, band < bands - 2]
    offsets = [-1, -2, 1, 2]
    below, above = group >= 1, group < groups - 1

    barrier = pltpu.get_barrier_semaphore()
    expected = jnp.int32(0)
    for ok, off in zip(has, offsets):
        expected += jnp.where(ok, 1, 0)

        @pl.when(ok)
        def _():
            pl.semaphore_signal(barrier, inc=1, device_id=(group, band + off), device_id_type=MESH)
    for ok, off in ((below, -1), (above, 1)):
        expected += jnp.where(ok, 1, 0)

        @pl.when(ok)
        def _():
            pl.semaphore_signal(barrier, inc=1, device_id=(group + off, band), device_id_type=MESH)

    loads = [pltpu.make_async_copy(x_hbm.at[j], xv.at[j], in_sem.at[j]) for j in range(slots)]
    for c in loads:
        c.start()

    size = fwd.shape[0]
    quarter = size // 4
    i0 = lax.broadcasted_iota(jnp.int32, (size, size), 0)
    i1 = lax.broadcasted_iota(jnp.int32, (size, size), 1)
    fwd[...] = jnp.where(i0 == 4 * (i1 % quarter) + i1 // quarter, 1.0, 0.0).astype(jnp.bfloat16)
    inv[...] = jnp.where(i1 == 4 * (i0 % quarter) + i0 // quarter, 1.0, 0.0).astype(jnp.bfloat16)

    first = group * slots
    total = jnp.int32(0)
    ancestor = [jnp.int32(0)] * slots
    for i in range(counts.shape[0]):
        total = total + counts[i]
        for j in range(slots):
            ancestor[j] = ancestor[j] + jnp.where(total <= first + j, 1, 0)
    local = [jnp.clip(a - first, 0, slots - 1) for a in ancestor]

    zero = lambda ref, lo, n: ref.__setitem__(pl.ds(lo, n), jnp.zeros((n,) + ref.shape[1:], jnp.float32))

    @pl.when(band == 0)
    def _():
        zero(q, 0, H0)
        zero(s1, 0, 3)
        zero(s2, HC - rows2, rows2)

    @pl.when(band <= 1)
    def _():
        zero(s2, HC - 2 * rows2, rows2)

    @pl.when(band == bands - 1)
    def _():
        zero(q, H0 + rows, H0)
        zero(s1, H1 + rows1 + 2, 3)
        zero(s2, HC + rows2, rows2)

    @pl.when(band >= bands - 2)
    def _():
        zero(s2, HC + 2 * rows2, rows2)

    for c in loads:
        c.wait()

    blocks = xv.shape[-1] // size
    for kb in range(blocks):
        cols = pl.ds(kb * size, size)
        a = jnp.concatenate([xv[local[s], l, :, cols] for l in range(2) for s in range(slots)], axis=0)
        hi = a.astype(jnp.bfloat16)
        lo = (a - hi.astype(jnp.float32)).astype(jnp.bfloat16)
        o = jnp.dot(hi, fwd[...], preferred_element_type=jnp.float32)
        o = o + jnp.dot(lo, fwd[...], preferred_element_type=jnp.float32)
        for r in range(4):
            tr[r, kb] = o[:, r * quarter:(r + 1) * quarter]

    lanes = blocks * quarter
    for y in range(rows):
        for r in range(4):
            for kb in range(blocks):
                q[H0 + y, r, :, kb * quarter:(kb + 1) * quarter] = tr[r, kb, pl.ds(y, 8, stride=rows), :]

    pl.semaphore_wait(barrier, expected)

    def remote(src, dst, sem, dev):
        return pltpu.make_async_remote_copy(
            src_ref=src, dst_ref=dst, send_sem=send_sem.at[sem], recv_sem=recv_sem.at[sem],
            device_id=dev, device_id_type=MESH)

    halo_down = remote(q.at[pl.ds(H0, H0)], q.at[pl.ds(H0 + rows, H0)], 0, (group, band - 1))
    halo_up = remote(q.at[pl.ds(rows, H0)], q.at[pl.ds(0, H0)], 1, (group, band + 1))
    pl.when(has[0])(halo_down.start)
    pl.when(has[2])(halo_up.start)

    sub = lax.broadcasted_iota(jnp.int32, (8, lanes), 0) >= slots
    sgn = jnp.where(sub, -1.0, 1.0).astype(jnp.float32)

    def diag(level):
        d = jnp.where(sub, 4.0 + DEFORM * 4.0 ** level, 4.0).astype(jnp.float32)
        return d, RELAX / d

    def swap(v):
        return pltpu.roll(v, slots, axis=0)

    def get(ref, i):
        return [ref[i, r] for r in range(ref.shape[1])]

    def put(ref, i, vals, mask):
        for r, v in enumerate(vals):
            ref[i, r] = v if mask is None else v * mask

    top = jnp.where(band == 0, 0.0, 1.0).astype(jnp.float32)
    bot = jnp.where(band == bands - 1, 0.0, 1.0).astype(jnp.float32)

    def over(lo, n, hi, body, unroll=2):
        for a, b, mask, u in ((lo, 0, top, 1), (0, n, None, unroll), (n, hi, bot, 1)):
            if b > a:
                def step(i, carry, mask=mask):
                    body(i, mask)
                    return carry
                lax.fori_loop(a, b, step, 0, unroll=u)

    pl.when(has[2])(halo_down.wait_recv)
    pl.when(has[0])(halo_up.wait_recv)

    d0, w0 = diag(0)

    def source(i, mask):
        row = get(q, H0 + i)
        put(s0, H0 + i, [-0.5 * (swap(v) + sgn * v) for v in row], None)
    over(-H0, rows, rows + H0, source)

    def pre(s_ref, f_ref, off, w):
        wa, wb = 1.2 * w, w * w

        def body(i, mask):
            row = get(s_ref, off + i)
            n = nb(get(s_ref, off + i - 1), row, get(s_ref, off + i + 1))
            put(f_ref, off + i, [wa * s + wb * v for s, v in zip(row, n)], mask)
        return body

    over(-5, rows, rows + 5, pre(s0, f0, H0, w0))

    def residual(s_ref, f_ref, off, d):
        def rest(i):
            row = get(f_ref, off + i)
            n = nb(get(f_ref, off + i - 1), row, get(f_ref, off + i + 1))
            return [s - d * f + v for s, f, v in zip(get(s_ref, off + i), row, n)]

        def coarse(i):
            a, b = rest(2 * i), rest(2 * i + 1)
            c = [x + y for x, y in zip(a, b)]
            return [c[2 * r] + c[2 * r + 1] for r in range(len(c) // 2)]
        return coarse

    coarse0 = residual(s0, f0, H0, d0)
    over(-2, rows1, rows1 + 2, lambda i, mask: put(s1, H1 + i, coarse0(i), mask), 1)

    one_down = remote(s1.at[pl.ds(H1 + 2, 3)], s1.at[pl.ds(H1 + rows1 + 2, 3)], 2, (group, band - 1))
    one_up = remote(s1.at[pl.ds(H1 + rows1 - 5, 3)], s1.at[pl.ds(0, 3)], 3, (group, band + 1))
    pl.when(has[0])(one_down.start)
    pl.when(has[2])(one_up.start)

    d1, w1 = diag(1)
    pre1 = pre(s1, f1, H1, w1)
    over(-1, rows1, rows1 + 1, pre1)
    coarse1 = residual(s1, f1, H1, d1)
    over(0, rows2, rows2, lambda i, mask: put(s2, HC + i, coarse1(i), mask), 1)

    own2 = s2.at[pl.ds(HC, rows2)]
    gather = []
    for n, (ok, off) in enumerate(zip(has, offsets)):
        c = remote(own2, s2.at[pl.ds(HC - off * rows2, rows2)], 4 + n, (group, band + off))
        pl.when(ok)(c.start)
        gather.append(c)

    pl.when(has[2])(one_down.wait_recv)
    pl.when(has[0])(one_up.wait_recv)

    def outer(a, b, mask):
        def step(i, carry):
            pre1(i, mask)
            return carry
        lax.fori_loop(a, b, step, 0)
    outer(-4, -1, top)
    outer(rows1 + 1, rows1 + 4, bot)

    for n, src in enumerate((2, 3, 0, 1)):
        pl.when(has[src])(gather[n].wait_recv)

    d2, w2 = diag(2)
    far_top = jnp.where(band <= 1, 0.0, 1.0).astype(jnp.float32)
    far_bot = jnp.where(band >= bands - 2, 0.0, 1.0).astype(jnp.float32)

    def mask2(i):
        if i < 0:
            return top if i >= -rows2 else far_top
        if i >= rows2:
            return bot if i < 2 * rows2 else far_bot
        return None

    body = pre(s2, c2a, HC, w2)
    for i in range(-6, rows2 + 6):
        body(i, mask2(i))

    def sweep(s_ref, f_ref, o_ref, off, w):
        def body(i, mask):
            row = get(f_ref, off + i)
            n = nb(get(f_ref, off + i - 1), row, get(f_ref, off + i + 1))
            put(o_ref, off + i, [0.2 * f + w * (s + v) for s, f, v in zip(get(s_ref, off + i), row, n)], mask)
        return body

    a, b = c2a, c2b
    for reach in (5, 4, 3, 2):
        body = sweep(s2, a, b, HC, w2)
        for i in range(-reach, rows2 + reach):
            body(i, mask2(i))
        a, b = b, a
    e2 = a

    def add1(i, mask):
        for t in range(2):
            e = e2[HC + i, 0]
            put(g1, H1 + 2 * i + t, [v + e for v in get(f1, H1 + 2 * i + t)], None)
    over(-2, rows2, rows2 + 2, add1)
    over(-3, rows1, rows1 + 3, sweep(s1, g1, h1, H1, w1))
    over(-2, rows1, rows1 + 2, sweep(s1, h1, g1, H1, w1))

    def add0(i, mask):
        e = get(g1, H1 + i)
        for t in range(2):
            v = get(f0, H0 + 2 * i + t)
            put(g0, H0 + 2 * i + t, [v[r] + e[r // 2] for r in range(4)], None)
    over(-2, rows1, rows1 + 2, add0)
    over(-2, rows, rows + 2, sweep(s0, g0, h0, H0, w0))
    last = sweep(s0, h0, g0, H0, w0)
    over(-1, rows, rows + 1, last)

    def to_stream(i, mask):
        put(h0, H0 + i, [swap(v) + sgn * v for v in get(g0, H0 + i)], None)
    over(-1, rows, rows + 1, to_stream)

    drag = jnp.where(sub, DRAG, 0.0).astype(jnp.float32)

    def advance(i, mask):
        st, su, sd = get(h0, H0 + i), get(h0, H0 + i - 1), get(h0, H0 + i + 1)
        qq, qu, qd = get(q, H0 + i), get(q, H0 + i - 1), get(q, H0 + i + 1)
        sl, sr = sides(st)
        ql, qr = sides(qq)
        for r in range(4):
            sx = 0.5 * (sr[r] - sl[r])
            sy = 0.5 * (sd[r] - su[r])
            qx = 0.5 * (qr[r] - ql[r])
            qy = 0.5 * (qd[r] - qu[r])
            lap = WY * (su[r] + sd[r]) + WX * (sl[r] + sr[r]) - 4.0 * st[r]
            v = qq[r] - STEP * (sx * qy - sy * qx + BETA * sx + drag * lap)
            for kb in range(blocks):
                tr[r, kb, pl.ds(i, 8, stride=rows), :] = v[:, kb * quarter:(kb + 1) * quarter]
    over(0, rows, rows, advance, 1)

    for kb in range(blocks):
        a = jnp.concatenate([tr[r, kb] for r in range(4)], axis=1)
        hi = a.astype(jnp.bfloat16)
        lo = (a - hi.astype(jnp.float32)).astype(jnp.bfloat16)
        o = jnp.dot(hi, inv[...], preferred_element_type=jnp.float32)
        o = o + jnp.dot(lo, inv[...], preferred_element_type=jnp.float32)
        for l in range(2):
            for s in range(slots):
                n = (l * slots + s) * rows
                ov[s, l, :, kb * size:(kb + 1) * size] = o[n:n + rows]

    share = remote(ov.at[slots - 1], out_hbm.at[0], 8, (group + 1, band))
    pl.when(above)(share.start)
    stores = [pltpu.make_async_copy(ov.at[j], out_hbm.at[j], out_sem.at[j]) for j in range(slots)]
    for c in stores[1:]:
        c.start()
    pl.when(group == 0)(stores[0].start)
    for c in stores[1:]:
        c.wait()
    pl.when(group == 0)(stores[0].wait)
    for ok, c in ((has[0], halo_down), (has[2], halo_up), (has[0], one_down), (has[2], one_up),
                  (above, share), *zip(has, gather)):
        pl.when(ok)(c.wait_send)
    pl.when(below)(share.wait_recv)


def per_device(states, counts):
    slots, layers, rows, nx = states.shape
    bands, groups = lax.axis_size("band"), lax.axis_size("particle")
    rows1, rows2, lanes = rows // 2, rows // 4, nx // 4
    f32 = jnp.float32
    level0 = pltpu.VMEM((rows + 2 * H0, 4, 8, lanes), f32)
    level1 = pltpu.VMEM((rows1 + 2 * H1, 2, 8, lanes), f32)
    level2 = pltpu.VMEM((rows2 + 2 * HC, 1, 8, lanes), f32)
    return pl.pallas_call(
        functools.partial(kernel, bands, groups, slots, rows),
        out_shape=jax.ShapeDtypeStruct(states.shape, states.dtype),
        in_specs=[pl.BlockSpec(memory_space=pltpu.SMEM), pl.BlockSpec(memory_space=pl.ANY)],
        out_specs=pl.BlockSpec(memory_space=pl.ANY),
        scratch_shapes=[
            pltpu.VMEM(states.shape, f32),
            pltpu.VMEM(states.shape, f32),
            pltpu.VMEM((512, 512), jnp.bfloat16),
            pltpu.VMEM((512, 512), jnp.bfloat16),
            pltpu.VMEM((4, nx // 512, 8 * rows, 128), f32),
            level0, level0, level0, level0, level0,
            level1, level1, level1, level1,
            level2, level2, level2,
            pltpu.SemaphoreType.DMA((slots,)),
            pltpu.SemaphoreType.DMA((slots,)),
            pltpu.SemaphoreType.DMA((9,)),
            pltpu.SemaphoreType.DMA((9,)),
        ],
        compiler_params=pltpu.CompilerParams(
            collective_id=0, has_side_effects=True, vmem_limit_bytes=40 * 1024 * 1024
        ),
    )(counts, states)


def solution(mesh):
    in_specs = (P("particle", None, "band", None), P())
    out_specs = P("particle", None, "band", None)
    return jax.shard_map(
        per_device, mesh=mesh, in_specs=in_specs, out_specs=out_specs, check_vma=False
    )
```

time: 146 us -> 26.3 us (0.18)
  starting transfers between devices: 42.4 us -> 0 us
  local copies, waits for them, and re-layouts: 37.7 us -> 2.49 us
  other arithmetic: 31.1 us -> 0 us
  waiting for transfers between devices: 27.8 us -> 0 us
  Pallas kernels: 0 us -> 23.6 us
  blocking collectives: 5.8 us -> 0 us
    ppermute x19 -> x0, starting transfers between devices: 42.4 us -> none  [the longest x9 21.6 us: padded(): lax.ppermute(tail, axis, [(i, (i + 1) % count) for i in range(ends)])]
    ppermute x19 -> x0, waiting for transfers between devices: 27.8 us -> none  [the longest x9 24.3 us: padded(): lax.ppermute(tail, axis, [(i, (i + 1) % count) for i in range(ends)])]
    reduce_sum x3 -> x0, other arithmetic: 23.6 us -> none  [the longest x2 23.4 us: restrict(): return jnp.sum(blocks, axis=(-3, -1))]
    pallas_call x0 -> x1, Pallas kernels: none -> 23.6 us  [per_device(): pl.pallas_call(functools.partial(kernel, bands, groups, slots, rows), out...]
    sub x2 -> x0, local copies, waits for them, and re-layouts: 11.3 us -> none  [cycle(): forcing_term - (diagonal_term * field - neighbours(field, strip_row_count...]
    reshape x4 -> x0, local copies, waits for them, and re-layouts: 8.08 us -> none  [prolong(): return jnp.repeat(jnp.repeat(field, 2, axis=-2), 2, axis=-1)]
    broadcast_in_dim x4 -> x0, local copies, waits for them, and re-layouts: 7.81 us -> none  [prolong(): return jnp.repeat(jnp.repeat(field, 2, axis=-2), 2, axis=-1)]
    all_gather x1 -> x0, blocking collectives: 5.8 us -> none  [coarse_level(): whole_column = lax.all_gather(forcing_term, 'band', axis=2, tiled=True)]
  transfers between devices with their start and end apart: 19 -> 0, of which waited for: 10 -> 0; matrix products, arithmetic and copies ran while one was open for 1% -> 0% of each run, Pallas kernels for 0% -> 0%
where the time goes in v1:
time: 26.3 us; the launch traced here: 26.1 us
  Pallas kernels  23.6 us (90%)
  local copies, waits for them, and re-layouts  2.49 us (9%)
    pallas_call x1, Pallas kernels, per_device(): pl.pallas_call(functools.partial(kernel, bands, groups, slots, rows), out...  23.6 us
    unnamed x5, local copies, waits for them, and re-layouts  2.49 us

profile of v1, /device:TPU:20, one launch (start us, length us, event | category | flops | bytes accessed | tf_op | source)
XLA Modules:
  0.0 26.1 jit_solution(12845857568400398273)
XLA Ops:
  0.0 0.0 copy-start
  0.0 1.0 %copy-done = f32[4,2,16,1024]{3,2,1,0:T(8,128)S(1)} copy-done((f32[4,2,16,1024]{3,2,1,0:T(8,128)S(1)}, f32[4,2,16,1024]{3,2,1,0:T(8,128)}, u32[]{:S(2)}) %copy-start) | copy-done | bytes 524312
  1.0 0.0 copy-start.1
  1.0 0.7 %copy-done.1 = s32[32]{0:T(128)S(1)} copy-done((s32[32]{0:T(128)S(1)}, s32[32]{0:T(128)}, u32[]{:S(2)}) %copy-start.1) | copy-done | bytes 152
  1.7 23.6 %shard_map.28 = f32[4,2,16,1024]{3,2,1,0:T(8,128)S(1)} custom-call(s32[32]{0:T(128)S(1)} %copy-done.1, f32[4,2,16,1024]{3,2,1,0:T(8,128)S(1)} %copy-done), custom_call_target="tpu_custom_call" | custom-call | tf_op jit(solution)/shard_map/pallas_call | solution.py:340
  25.3 0.8 %copy.4 = f32[4,2,16,1024]{3,2,1,0:T(8,128)} copy(f32[4,2,16,1024]{3,2,1,0:T(8,128)S(1)} %shard_map.28) | data formatting | bytes 1048576
Async XLA Ops:
  0.0 1.0 %copy-start = (f32[4,2,16,1024]{3,2,1,0:T(8,128)S(1)}, f32[4,2,16,1024]{3,2,1,0:T(8,128)}, u32[]{:S(2)}) copy-start(f32[4,2,16,1024]{3,2,1,0:T(8,128)} %x_hbm.1) | copy-start | bytes 1572868
  1.0 0.7 %copy-start.1 = (s32[32]{0:T(128)S(1)}, s32[32]{0:T(128)}, u32[]{:S(2)}) copy-start(s32[32]{0:T(128)} %counts.1) | copy-start | bytes 388

commit v2 on v1

--- a/solution.py
+++ b/solution.py
@@ -39,7 +39,7 @@
 
 
 def kernel(bands, groups, slots, rows, counts, x_hbm, out_hbm,
-           xv, ov, fwd, inv, tr, q, s0, f0, g0, h0, s1, f1, g1, h1, s2, c2a, c2b,
+           xv, ov, fwd, inv, tr, q, s0, f0, g0, h0, st0, s1, f1, g1, h1, s2, c2a, c2b,
            in_sem, out_sem, send_sem, recv_sem):
     band = lax.axis_index("band")
     group = lax.axis_index("particle")
@@ -157,23 +157,24 @@
     top = jnp.where(band == 0, 0.0, 1.0).astype(jnp.float32)
     bot = jnp.where(band == bands - 1, 0.0, 1.0).astype(jnp.float32)
 
-    def over(lo, n, hi, body, unroll=2):
-        for a, b, mask, u in ((lo, 0, top, 1), (0, n, None, unroll), (n, hi, bot, 1)):
+    def over(lo, n, hi, body, unroll=4):
+        parts = ((lo, min(hi, 0), top, True), (max(lo, 0), min(hi, n), None, unroll),
+                 (max(lo, n), hi, bot, True))
+        for a, b, mask, u in parts:
             if b > a:
                 def step(i, carry, mask=mask):
                     body(i, mask)
                     return carry
+                if u is not True:
+                    u = max(k for k in range(1, u + 1) if (b - a) % k == 0)
                 lax.fori_loop(a, b, step, 0, unroll=u)
-
-    pl.when(has[2])(halo_down.wait_recv)
-    pl.when(has[0])(halo_up.wait_recv)
 
     d0, w0 = diag(0)
 
     def source(i, mask):
         row = get(q, H0 + i)
         put(s0, H0 + i, [-0.5 * (swap(v) + sgn * v) for v in row], None)
-    over(-H0, rows, rows + H0, source)
+    over(0, rows, rows, source)
 
     def pre(s_ref, f_ref, off, w):
         wa, wb = 1.2 * w, w * w
@@ -184,7 +185,8 @@
             put(f_ref, off + i, [wa * s + wb * v for s, v in zip(row, n)], mask)
         return body
 
-    over(-5, rows, rows + 5, pre(s0, f0, H0, w0))
+    pre0 = pre(s0, f0, H0, w0)
+    over(1, rows, rows - 1, pre0)
 
     def residual(s_ref, f_ref, off, d):
         def rest(i):
@@ -199,7 +201,17 @@
         return coarse
 
     coarse0 = residual(s0, f0, H0, d0)
-    over(-2, rows1, rows1 + 2, lambda i, mask: put(s1, H1 + i, coarse0(i), mask), 1)
+    right1 = lambda i, mask: put(s1, H1 + i, coarse0(i), mask)
+    over(1, rows1, rows1 - 1, right1, 2)
+
+    pl.when(has[2])(halo_down.wait_recv)
+    pl.when(has[0])(halo_up.wait_recv)
+    over(-H0, rows, 0, source)
+    over(rows, rows, rows + H0, source)
+    over(-5, rows, 1, pre0)
+    over(rows - 1, rows, rows + 5, pre0)
+    over(-2, rows1, 1, right1)
+    over(rows1 - 1, rows1, rows1 + 2, right1)
 
     one_down = remote(s1.at[pl.ds(H1 + 2, 3)], s1.at[pl.ds(H1 + rows1 + 2, 3)], 2, (group, band - 1))
     one_up = remote(s1.at[pl.ds(H1 + rows1 - 5, 3)], s1.at[pl.ds(0, 3)], 3, (group, band + 1))
@@ -208,9 +220,9 @@
 
     d1, w1 = diag(1)
     pre1 = pre(s1, f1, H1, w1)
-    over(-1, rows1, rows1 + 1, pre1)
+    over(-1, rows1, rows1 + 1, pre1, 8)
     coarse1 = residual(s1, f1, H1, d1)
-    over(0, rows2, rows2, lambda i, mask: put(s2, HC + i, coarse1(i), mask), 1)
+    over(0, rows2, rows2, lambda i, mask: put(s2, HC + i, coarse1(i), mask), 4)
 
     own2 = s2.at[pl.ds(HC, rows2)]
     gather = []
@@ -226,7 +238,7 @@
         def step(i, carry):
             pre1(i, mask)
             return carry
-        lax.fori_loop(a, b, step, 0)
+        lax.fori_loop(a, b, step, 0, unroll=True)
     outer(-4, -1, top)
     outer(rows1 + 1, rows1 + 4, bot)
 
@@ -268,8 +280,8 @@
             e = e2[HC + i, 0]
             put(g1, H1 + 2 * i + t, [v + e for v in get(f1, H1 + 2 * i + t)], None)
     over(-2, rows2, rows2 + 2, add1)
-    over(-3, rows1, rows1 + 3, sweep(s1, g1, h1, H1, w1))
-    over(-2, rows1, rows1 + 2, sweep(s1, h1, g1, H1, w1))
+    over(-3, rows1, rows1 + 3, sweep(s1, g1, h1, H1, w1), 8)
+    over(-2, rows1, rows1 + 2, sweep(s1, h1, g1, H1, w1), 8)
 
     def add0(i, mask):
         e = get(g1, H1 + i)
@@ -277,18 +289,18 @@
             v = get(f0, H0 + 2 * i + t)
             put(g0, H0 + 2 * i + t, [v[r] + e[r // 2] for r in range(4)], None)
     over(-2, rows1, rows1 + 2, add0)
-    over(-2, rows, rows + 2, sweep(s0, g0, h0, H0, w0))
-    last = sweep(s0, h0, g0, H0, w0)
-    over(-1, rows, rows + 1, last)
+    first0 = sweep(s0, g0, h0, H0, w0)
+    last0 = sweep(s0, h0, g0, H0, w0)
 
     def to_stream(i, mask):
-        put(h0, H0 + i, [swap(v) + sgn * v for v in get(g0, H0 + i)], None)
-    over(-1, rows, rows + 1, to_stream)
+        put(st0, H0 + i, [swap(v) + sgn * v for v in get(g0, H0 + i)], None)
 
     drag = jnp.where(sub, DRAG, 0.0).astype(jnp.float32)
 
-    def advance(i, mask):
-        st, su, sd = get(h0, H0 + i), get(h0, H0 + i - 1), get(h0, H0 + i + 1)
+    part = 8
+
+    def advance(base, i, mask):
+        st, su, sd = get(st0, H0 + i), get(st0, H0 + i - 1), get(st0, H0 + i + 1)
         qq, qu, qd = get(q, H0 + i), get(q, H0 + i - 1), get(q, H0 + i + 1)
         sl, sr = sides(st)
         ql, qr = sides(qq)
@@ -300,33 +312,47 @@
             lap = WY * (su[r] + sd[r]) + WX * (sl[r] + sr[r]) - 4.0 * st[r]
             v = qq[r] - STEP * (sx * qy - sy * qx + BETA * sx + drag * lap)
             for kb in range(blocks):
-                tr[r, kb, pl.ds(i, 8, stride=rows), :] = v[:, kb * quarter:(kb + 1) * quarter]
-    over(0, rows, rows, advance, 1)
-
-    for kb in range(blocks):
-        a = jnp.concatenate([tr[r, kb] for r in range(4)], axis=1)
-        hi = a.astype(jnp.bfloat16)
-        lo = (a - hi.astype(jnp.float32)).astype(jnp.bfloat16)
-        o = jnp.dot(hi, inv[...], preferred_element_type=jnp.float32)
-        o = o + jnp.dot(lo, inv[...], preferred_element_type=jnp.float32)
-        for l in range(2):
-            for s in range(slots):
-                n = (l * slots + s) * rows
-                ov[s, l, :, kb * size:(kb + 1) * size] = o[n:n + rows]
-
-    share = remote(ov.at[slots - 1], out_hbm.at[0], 8, (group + 1, band))
-    pl.when(above)(share.start)
-    stores = [pltpu.make_async_copy(ov.at[j], out_hbm.at[j], out_sem.at[j]) for j in range(slots)]
-    for c in stores[1:]:
-        c.start()
-    pl.when(group == 0)(stores[0].start)
-    for c in stores[1:]:
-        c.wait()
-    pl.when(group == 0)(stores[0].wait)
+                tr[r, kb, pl.ds(base + i, 8, stride=part), :] = v[:, kb * quarter:(kb + 1) * quarter]
+    made = [-2, -1, 0]
+    shares, stores = [], []
+    for c in range(rows // part):
+        end = (c + 1) * part
+        over(made[0], rows, end + 2, first0)
+        over(made[1], rows, end + 1, last0)
+        over(made[1], rows, end + 1, to_stream)
+        base = c * part * 7
+        over(made[2], rows, end, functools.partial(advance, base), 2)
+        made = [end + 2, end + 1, end]
+        m = pl.ds(c * part * 8, part * 8)
+        here = pl.ds(c * part, part)
+        for kb in range(blocks):
+            a = jnp.concatenate([tr[r, kb, m] for r in range(4)], axis=1)
+            hi = a.astype(jnp.bfloat16)
+            lo = (a - hi.astype(jnp.float32)).astype(jnp.bfloat16)
+            o = jnp.dot(hi, inv[...], preferred_element_type=jnp.float32)
+            o = o + jnp.dot(lo, inv[...], preferred_element_type=jnp.float32)
+            for l in range(2):
+                for s in range(slots):
+                    n = (l * slots + s) * part
+                    ov[s, l, here, kb * size:(kb + 1) * size] = o[n:n + part]
+        share = remote(ov.at[slots - 1, :, here], out_hbm.at[0, :, here], 8 + c, (group + 1, band))
+        pl.when(above)(share.start)
+        shares.append((above, share))
+        own = pl.ds(1, slots - 1)
+        keep = pltpu.make_async_copy(ov.at[own, :, here], out_hbm.at[own, :, here], out_sem.at[2 * c])
+        keep.start()
+        lone = pltpu.make_async_copy(ov.at[0, :, here], out_hbm.at[0, :, here], out_sem.at[2 * c + 1])
+        pl.when(group == 0)(lone.start)
+        stores.append((keep, lone))
+
+    for keep, lone in stores:
+        keep.wait()
+        pl.when(group == 0)(lone.wait)
     for ok, c in ((has[0], halo_down), (has[2], halo_up), (has[0], one_down), (has[2], one_up),
-                  (above, share), *zip(has, gather)):
+                  *shares, *zip(has, gather)):
         pl.when(ok)(c.wait_send)
-    pl.when(below)(share.wait_recv)
+    for _, c in shares:
+        pl.when(below)(c.wait_recv)
 
 
 def per_device(states, counts):
@@ -348,16 +374,16 @@
             pltpu.VMEM((512, 512), jnp.bfloat16),
             pltpu.VMEM((512, 512), jnp.bfloat16),
             pltpu.VMEM((4, nx // 512, 8 * rows, 128), f32),
-            level0, level0, level0, level0, level0,
+            level0, level0, level0, level0, level0, level0,
             level1, level1, level1, level1,
             level2, level2, level2,
             pltpu.SemaphoreType.DMA((slots,)),
-            pltpu.SemaphoreType.DMA((slots,)),
-            pltpu.SemaphoreType.DMA((9,)),
-            pltpu.SemaphoreType.DMA((9,)),
+            pltpu.SemaphoreType.DMA((rows // 4,)),
+            pltpu.SemaphoreType.DMA((8 + rows // 8,)),
+            pltpu.SemaphoreType.DMA((8 + rows // 8,)),
         ],
         compiler_params=pltpu.CompilerParams(
-            collective_id=0, has_side_effects=True, vmem_limit_bytes=40 * 1024 * 1024
+            collective_id=0, has_side_effects=True, vmem_limit_bytes=64 * 1024 * 1024 - 256 * 1024
         ),
     )(counts, states)
 

time: 26.3 us -> 20.7 us (0.79)
  Pallas kernels: 23.6 us -> 18.6 us
  local copies, waits for them, and re-layouts: 2.49 us -> 1.89 us
    pallas_call x1, Pallas kernels: 23.6 us -> 18.6 us  [per_device(): pl.pallas_call(functools.partial(kernel, bands, groups, slots, rows), out...]
    unnamed x5 -> x1, local copies, waits for them, and re-layouts: 2.49 us -> 1.89 us
where the time goes in v2:
time: 20.7 us; the launch traced here: 20.5 us
  Pallas kernels  18.6 us (90%)
  local copies, waits for them, and re-layouts  1.89 us (9%)
    pallas_call x1, Pallas kernels, per_device(): pl.pallas_call(functools.partial(kernel, bands, groups, slots, rows), out...  18.6 us
    unnamed x1, local copies, waits for them, and re-layouts  1.89 us

profile of v2, /device:TPU:20, one launch (start us, length us, event | category | flops | bytes accessed | tf_op | source)
XLA Modules:
  0.0 20.5 jit_solution(10637005674064229960)
XLA Ops:
  0.0 18.6 %shard_map.28 = f32[4,2,16,1024]{3,2,1,0:T(8,128)} custom-call(s32[32]{0:T(128)} %counts.1, f32[4,2,16,1024]{3,2,1,0:T(8,128)} %x_hbm.1), custom_call_target="tpu_custom_call" | custom-call | tf_op jit(solution)/shard_map/pallas_call | solution.py:366
  18.6 1.9 %copy.4 = f32[4,2,16,1024]{3,2,1,0:T(8,128)} copy(f32[4,2,16,1024]{3,2,1,0:T(8,128)} %shard_map.28) | data formatting | bytes 1048576

commit v3 on v2

--- a/solution.py
+++ b/solution.py
@@ -132,10 +132,18 @@
             src_ref=src, dst_ref=dst, send_sem=send_sem.at[sem], recv_sem=recv_sem.at[sem],
             device_id=dev, device_id_type=MESH)
 
-    halo_down = remote(q.at[pl.ds(H0, H0)], q.at[pl.ds(H0 + rows, H0)], 0, (group, band - 1))
-    halo_up = remote(q.at[pl.ds(rows, H0)], q.at[pl.ds(0, H0)], 1, (group, band + 1))
-    pl.when(has[0])(halo_down.start)
-    pl.when(has[2])(halo_up.start)
+    half = H0 // 2
+    spare = 8 + rows // 8
+    halos_down, halos_up = [], []
+    for k in range(2):
+        lo = H0 + k * half
+        hi = H0 + rows - (k + 1) * half
+        d = remote(q.at[pl.ds(lo, half)], q.at[pl.ds(lo + rows, half)], (0, spare)[k], (group, band - 1))
+        u = remote(q.at[pl.ds(hi, half)], q.at[pl.ds(hi - rows, half)], (1, spare + 1)[k], (group, band + 1))
+        pl.when(has[0])(d.start)
+        pl.when(has[2])(u.start)
+        halos_down.append(d)
+        halos_up.append(u)
 
     sub = lax.broadcasted_iota(jnp.int32, (8, lanes), 0) >= slots
     sgn = jnp.where(sub, -1.0, 1.0).astype(jnp.float32)
@@ -204,8 +212,9 @@
     right1 = lambda i, mask: put(s1, H1 + i, coarse0(i), mask)
     over(1, rows1, rows1 - 1, right1, 2)
 
-    pl.when(has[2])(halo_down.wait_recv)
-    pl.when(has[0])(halo_up.wait_recv)
+    for d, u in zip(halos_down, halos_up):
+        pl.when(has[2])(d.wait_recv)
+        pl.when(has[0])(u.wait_recv)
     over(-H0, rows, 0, source)
     over(rows, rows, rows + H0, source)
     over(-5, rows, 1, pre0)
@@ -224,10 +233,12 @@
     coarse1 = residual(s1, f1, H1, d1)
     over(0, rows2, rows2, lambda i, mask: put(s2, HC + i, coarse1(i), mask), 4)
 
-    own2 = s2.at[pl.ds(HC, rows2)]
     gather = []
     for n, (ok, off) in enumerate(zip(has, offsets)):
-        c = remote(own2, s2.at[pl.ds(HC - off * rows2, rows2)], 4 + n, (group, band + off))
+        skip = 1 if abs(off) == 2 else 0
+        src = skip if off > 0 else 0
+        c = remote(s2.at[pl.ds(HC + src, rows2 - skip)],
+                   s2.at[pl.ds(HC - off * rows2 + src, rows2 - skip)], 4 + n, (group, band + off))
         pl.when(ok)(c.start)
         gather.append(c)
 
@@ -348,7 +359,7 @@
     for keep, lone in stores:
         keep.wait()
         pl.when(group == 0)(lone.wait)
-    for ok, c in ((has[0], halo_down), (has[2], halo_up), (has[0], one_down), (has[2], one_up),
+    for ok, c in (*((has[0], d) for d in halos_down), *((has[2], u) for u in halos_up), (has[0], one_down), (has[2], one_up),
                   *shares, *zip(has, gather)):
         pl.when(ok)(c.wait_send)
     for _, c in shares:
@@ -379,8 +390,8 @@
             level2, level2, level2,
             pltpu.SemaphoreType.DMA((slots,)),
             pltpu.SemaphoreType.DMA((rows // 4,)),
-            pltpu.SemaphoreType.DMA((8 + rows // 8,)),
-            pltpu.SemaphoreType.DMA((8 + rows // 8,)),
+            pltpu.SemaphoreType.DMA((10 + rows // 8,)),
+            pltpu.SemaphoreType.DMA((10 + rows // 8,)),
         ],
         compiler_params=pltpu.CompilerParams(
             collective_id=0, has_side_effects=True, vmem_limit_bytes=64 * 1024 * 1024 - 256 * 1024

time: 20.7 us -> 20.6 us (level)
  no operation moved by 1% of the time
where the time goes in v3:
time: 20.6 us; the launch traced here: 20.4 us
  Pallas kernels  18.5 us (90%)
  local copies, waits for them, and re-layouts  1.89 us (9%)
    pallas_call x1, Pallas kernels, per_device(): pl.pallas_call(functools.partial(kernel, bands, groups, slots, rows), out...  18.5 us
    unnamed x1, local copies, waits for them, and re-layouts  1.89 us

profile of v3, /device:TPU:20, one launch (start us, length us, event | category | flops | bytes accessed | tf_op | source)
XLA Modules:
  0.0 20.4 jit_solution(4992923433272189087)
XLA Ops:
  0.0 18.5 %shard_map.28 = f32[4,2,16,1024]{3,2,1,0:T(8,128)} custom-call(s32[32]{0:T(128)} %counts.1, f32[4,2,16,1024]{3,2,1,0:T(8,128)} %x_hbm.1), custom_call_target="tpu_custom_call" | custom-call | tf_op jit(solution)/shard_map/pallas_call | solution.py:377
  18.5 1.9 %copy.4 = f32[4,2,16,1024]{3,2,1,0:T(8,128)} copy(f32[4,2,16,1024]{3,2,1,0:T(8,128)} %shard_map.28) | data formatting | bytes 1048576

commit v4 on v3

--- a/solution.py
+++ b/solution.py
@@ -212,20 +212,29 @@
     right1 = lambda i, mask: put(s1, H1 + i, coarse0(i), mask)
     over(1, rows1, rows1 - 1, right1, 2)
 
-    for d, u in zip(halos_down, halos_up):
-        pl.when(has[2])(d.wait_recv)
-        pl.when(has[0])(u.wait_recv)
-    over(-H0, rows, 0, source)
-    over(rows, rows, rows + H0, source)
-    over(-5, rows, 1, pre0)
-    over(rows - 1, rows, rows + 5, pre0)
-    over(-2, rows1, 1, right1)
-    over(rows1 - 1, rows1, rows1 + 2, right1)
-
+    def landed(k):
+        pl.when(has[2])(halos_down[k].wait_recv)
+        pl.when(has[0])(halos_up[k].wait_recv)
+
+    landed(0)
     one_down = remote(s1.at[pl.ds(H1 + 2, 3)], s1.at[pl.ds(H1 + rows1 + 2, 3)], 2, (group, band - 1))
     one_up = remote(s1.at[pl.ds(H1 + rows1 - 5, 3)], s1.at[pl.ds(0, 3)], 3, (group, band + 1))
     pl.when(has[0])(one_down.start)
     pl.when(has[2])(one_up.start)
+
+    over(-half, rows, 0, source)
+    over(rows, rows, rows + half, source)
+    over(1 - half, rows, 1, pre0)
+    over(rows - 1, rows, rows + half - 1, pre0)
+    over(0, rows1, 1, right1)
+    over(rows1 - 1, rows1, rows1, right1)
+    landed(1)
+    over(-H0, rows, -half, source)
+    over(rows + half, rows, rows + H0, source)
+    over(-5, rows, 1 - half, pre0)
+    over(rows + half - 1, rows, rows + 5, pre0)
+    over(-2, rows1, 0, right1)
+    over(rows1, rows1, rows1 + 2, right1)
 
     d1, w1 = diag(1)
     pre1 = pre(s1, f1, H1, w1)

time: 20.6 us -> 20.1 us (0.976)
  Pallas kernels: 18.5 us -> 18 us
    pallas_call x1, Pallas kernels: 18.5 us -> 18 us  [per_device(): pl.pallas_call(functools.partial(kernel, bands, groups, slots, rows), out...]
where the time goes in v4:
time: 20.1 us; the launch traced here: 19.9 us
  Pallas kernels  18 us (90%)
  local copies, waits for them, and re-layouts  1.89 us (9%)
    pallas_call x1, Pallas kernels, per_device(): pl.pallas_call(functools.partial(kernel, bands, groups, slots, rows), out...  18 us
    unnamed x1, local copies, waits for them, and re-layouts  1.89 us

profile of v4, /device:TPU:20, one launch (start us, length us, event | category | flops | bytes accessed | tf_op | source)
XLA Modules:
  0.0 19.9 jit_solution(11252358716635788928)
XLA Ops:
  0.0 18.0 %shard_map.28 = f32[4,2,16,1024]{3,2,1,0:T(8,128)} custom-call(s32[32]{0:T(128)} %counts.1, f32[4,2,16,1024]{3,2,1,0:T(8,128)} %x_hbm.1), custom_call_target="tpu_custom_call" | custom-call | tf_op jit(solution)/shard_map/pallas_call | solution.py:386
  18.0 1.9 %copy.4 = f32[4,2,16,1024]{3,2,1,0:T(8,128)} copy(f32[4,2,16,1024]{3,2,1,0:T(8,128)} %shard_map.28) | data formatting | bytes 1048576
